TPU v7x, 32 devices: a whole 2x2x4 slice. The times are simulated.
32 devices in a mesh: enc: 4 (over y, x), span: 8 (over z, core).
Axes of the slice: x: 2, y: 2, z: 4, core: 2. Of those that a mesh axis runs over, the one named last changes fastest.
Arguments:
- queries: bfloat16 [8192, 3072], P('span', 'enc'), may hold values from -6 to 6
- cotangent: bfloat16 [8192, 3072], P('span', 'enc'), may hold values from -12 to 12
- key_weight: bfloat16 [896, 3072], P(None, 'enc'), may hold values from -0.1875 to 0.1875
- value_weight: bfloat16 [896, 3072], P(None, 'enc'), may hold values from -0.75 to 0.75
- neighbour_store: bfloat16 [256, 128, 896], P('span', None, 'enc'), may hold values from -6 to 6
- block_scale: bfloat16 [256, 128], P('span'), may hold values from 0.5 to 2
- fetch_index: int32 [8, 8, 8], P('span'), may hold values from 0 to 31
- neighbour_slot: int32 [8, 32], P('span'), may hold values from 0 to 63, as said below
- second_valid: int32 [8, 16], P('span'), may hold values 0 or 1
- live_spans: int32 [8], P('span'), may hold values from 1 to 16, as said below
Outputs:
- attended: bfloat16 [8192, 3072], P('span', 'enc')
- grad_store: float32 [256, 128, 896], P('span', None, 'enc')
Inputs may be any that keep to these rules, and one draw needn't show every extreme that they name: `fetch_index`: the local block, of the 32 of store shard c2, that it sends to owner shard c in slot s; slots that no neighbour names are padding. `neighbour_slot`: entry j * 2 + k of row c names the fetched slot c2 * 8 + s holding neighbour k of owner shard c's span j; no slot is named twice in a row; the slots named from store shard c2 are c2 * 8 to c2 * 8 + n - 1 for some count n of 0 to 8; in each row one store shard gives all 8 slots, and each store shard gives all 8 slots to some owner shard. Spans 0 to live_spans[c] - 1 of owner shard c are live, the others are padding; some shard has all 16 live.
All inputs are finite; a program needn't handle non-finite values. No bound on the sum of `second_valid` on one device may be relied on, other than what follows from the above.
Results may differ from a plain program's by a relative error of at most 0.012.
The roundings to bfloat16 on the way count: a program that leaves them out, or rounds other values in their place, can miss the bound.
Values may be sent and summed in bfloat16 or wider, within the bound.
A program may use at most 192 MiB of HBM per device.

v0:
```python
import math

import jax
import jax.numpy as jnp
from jax import lax
from jax.sharding import PartitionSpec as P

HD = 128
CL = 64
NT = 128
NBR = 2


def attend_blocks(queries, cotangent, key_proj, value_proj, valid_row, live_count):
    spans = queries.shape[0] // CL
    heads_here = queries.shape[1] // HD
    query_view = queries.reshape(spans, CL, heads_here, HD)
    keys_view = key_proj.reshape(spans, NBR * NT, heads_here, HD)
    values_view = value_proj.reshape(spans, NBR * NT, heads_here, HD)
    scale_factor = 1.0 / math.sqrt(HD)
    neighbour = jnp.arange(NBR * NT, dtype=jnp.int32) // NT
    key_mask = jnp.where(neighbour[None, :] == 0, 1.0, valid_row[:, None].astype(jnp.float32))
    live_mask = jnp.arange(spans, dtype=jnp.int32) < live_count
    scores = (
        jnp.einsum("cqhd,ckhd->chqk", query_view, keys_view, preferred_element_type=jnp.float32)
        * scale_factor
    )
    weights = jnp.exp(scores) * key_mask[:, None, None, :]
    probabilities = weights / jnp.sum(weights, axis=-1, keepdims=True)
    probs_low = probabilities.astype(jnp.bfloat16)
    mixture = jnp.einsum(
        "chqk,ckhd->cqhd", probs_low, values_view, preferred_element_type=jnp.float32
    )
    attended = jnp.where(live_mask[:, None, None, None], mixture, 0.0).astype(jnp.bfloat16)
    grad_out = jnp.where(
        live_mask[:, None, None, None], cotangent.reshape(spans, CL, heads_here, HD), 0.0
    )
    grad_values = jnp.einsum(
        "chqk,cqhd->ckhd", probs_low, grad_out, preferred_element_type=jnp.float32
    ).astype(jnp.bfloat16)
    grad_probs = jnp.einsum(
        "cqhd,ckhd->chqk", grad_out, values_view, preferred_element_type=jnp.float32
    )
    inner_sum = jnp.sum(probabilities * grad_probs, axis=-1, keepdims=True)
    grad_scores = (probabilities * (grad_probs - inner_sum) * scale_factor).astype(jnp.bfloat16)
    grad_keys = jnp.einsum(
        "chqk,cqhd->ckhd", grad_scores, query_view, preferred_element_type=jnp.float32
    ).astype(jnp.bfloat16)
    head_width = heads_here * HD
    return (
        attended.reshape(queries.shape),
        grad_keys.reshape(-1, head_width),
        grad_values.reshape(-1, head_width),
    )


def per_device(
    queries,
    cotangent,
    key_weight,
    value_weight,
    neighbour_store,
    block_scale,
    fetch_index,
    neighbour_slot,
    second_valid,
    live_spans,
):
    enc_count = lax.axis_size("enc")
    shard_count = lax.axis_size("span")
    capacity = fetch_index.shape[2]
    blocks_here = neighbour_store.shape[0]
    features = neighbour_store.shape[2]
    head_width = key_weight.shape[1]
    slot_order = neighbour_slot[0]
    used_count = slot_order.shape[0]
    slot_total = shard_count * capacity
    served = fetch_index[0].reshape(slot_total)
    scale_wide = block_scale.astype(jnp.float32)
    encoded = (neighbour_store.astype(jnp.float32) * scale_wide[:, :, None]).astype(jnp.bfloat16)
    outgoing = jnp.take(encoded, served, axis=0)
    spread = jnp.broadcast_to(outgoing[None], (enc_count,) + outgoing.shape)
    spread = spread.reshape((enc_count * outgoing.shape[0],) + outgoing.shape[1:])
    received = lax.all_to_all(spread, ("enc", "span"), split_axis=0, concat_axis=0, tiled=True)
    received = received.reshape((enc_count, slot_total) + outgoing.shape[1:])
    arranged = jnp.take(received, slot_order, axis=1)
    key_stack = key_weight.reshape(enc_count, features, head_width)
    value_stack = value_weight.reshape(enc_count, features, head_width)
    key_total = jnp.einsum("esnf,efw->snw", arranged, key_stack, preferred_element_type=jnp.float32)
    value_total = jnp.einsum(
        "esnf,efw->snw", arranged, value_stack, preferred_element_type=jnp.float32
    )
    key_proj = key_total.astype(jnp.bfloat16).reshape(-1, head_width)
    value_proj = value_total.astype(jnp.bfloat16).reshape(-1, head_width)
    attended, grad_keys, grad_values = attend_blocks(
        queries, cotangent, key_proj, value_proj, second_valid[0], live_spans[0]
    )
    contract = (((1,), (1,)), ((), ()))
    selector = (
        served.reshape(shard_count, capacity)[None, :, :]
        == jnp.arange(blocks_here, dtype=jnp.int32)[:, None, None]
    ).astype(jnp.float32)
    key_term = lax.dot_general(key_weight, grad_keys, contract, preferred_element_type=jnp.float32)
    value_term = lax.dot_general(
        value_weight, grad_values, contract, preferred_element_type=jnp.float32
    )
    whole_grad = (key_term + value_term).astype(jnp.bfloat16)
    in_spans = whole_grad.reshape(enc_count * features, used_count, NT)
    by_slot = (
        jnp.zeros((enc_count * features, slot_total, NT), jnp.bfloat16)
        .at[:, slot_order]
        .set(in_spans)
    )
    grouped = by_slot.reshape(enc_count, features, shard_count, capacity * NT).transpose(0, 2, 1, 3)
    grouped = grouped.reshape(enc_count * shard_count, features, capacity * NT)
    arrived = lax.all_to_all(grouped, ("enc", "span"), split_axis=0, concat_axis=0, tiled=True)
    arriving = jnp.sum(
        arrived.astype(jnp.float32).reshape(enc_count, shard_count, features, capacity, NT), axis=0
    )
    grad_blocks = jnp.einsum("bcs,cfst->btf", selector, arriving, precision=lax.Precision.HIGHEST)
    grad_store = grad_blocks * scale_wide[:, :, None]
    return (attended, grad_store)


def solution(mesh):
    return jax.shard_map(
        per_device,
        mesh=mesh,
        in_specs=(
            P("span", "enc"),
            P("span", "enc"),
            P(None, "enc"),
            P(None, "enc"),
            P("span", None, "enc"),
            P("span", None),
            P("span", None, None),
            P("span", None),
            P("span", None),
            P("span"),
        ),
        out_specs=(P("span", "enc"), P("span", None, "enc")),
        check_vma=False,
    )
```

profile of v0, /device:TPU:0, one launch (start us, length us, event | category | flops | bytes accessed | tf_op | source)
XLA Modules:
  0.0 989.0 jit_solution(12105864147183295546)
XLA Ops:
  11.8 5.6 broadcast_in_dim.87
  17.4 7.6 all-to-all-start
  28.5 3.4 reshape.176
  33.6 311.1 %all-to-all-done = bf16[256,128,224]{1,2,0:T(8,128)(2,1)} async-done(((bf16[256,128,224]{1,2,0:T(8,128)(2,1)}), bf16[256,128,224]{1,2,0:T(8,128)(2,1)}, u32[]{:S(2)}, u32[]{:S(2)}) %all-to-all-start) | async-done | bytes 14680096 | tf_op jit(solution)/shard_map/all_to_all | solution.py:84
  344.7 9.6 gather_fusion.1
  354.3 14.8 %bitcast_convert_fusion = bf16[32,128,768]{2,1,0:T(8,128)(2,1)} fusion(bf16[4,224,768,1]{2,1,0,3:T(8,128)(2,1)S(1)} %bitcast.103, bf16[32,4,128,224]{2,3,1,0:T(8,128)(2,1)} %gather_fusion.1, pred[32]{0:T(512)(128)(4,1)S(1)} %compare_and_fusion.1), kind=kOutput, calls=%fused_computation.5 | convolution fusion | flops 5643960320 | bytes 15007776 | tf_op jit(solution)/shard_map/esnf,efw->snw/dot_general | solution.py:89
  369.2 9.7 bitcast_convert_fusion.1
  378.9 13.6 %reshape.217 = bf16[16,256,6,128]{3,2,1,0:T(8,128)(2,1)} reshape(bf16[32,128,768]{2,1,0:T(8,128)(2,1)} %bitcast_convert_fusion.1) | data formatting | bytes 12582912 | tf_op jit(solution)/shard_map/reshape;reshape | solution.py:19
  392.5 14.0 %reshape.216 = bf16[16,256,6,128]{3,2,1,0:T(8,128)(2,1)} reshape(bf16[32,128,768]{2,1,0:T(8,128)(2,1)} %bitcast_convert_fusion) | data formatting | bytes 12582912 | tf_op jit(solution)/shard_map/reshape;reshape | solution.py:18
  406.6 8.5 fusion.8
  415.1 6.6 bitcast_reduce_fusion
  422.3 6.0 convert_bitcast_fusion
  428.3 47.6 %convert_bitcast_fusion.1 = bf16[16,256,6,128]{3,1,2,0:T(8,128)(2,1)} fusion(f32[16,6,64,256]{3,2,1,0:T(8,128)} %fusion.8, bf16[16,64,6,128]{3,2,1,0:T(8,128)(2,1)} %reshape.174, f32[16,6,256,64]{2,3,1,0:T(8,128)} %get-tuple-element.9, f32[16,6,64]{2,1,0:T(8,128)} %copy-done.13, f32[16,256]{1,0:T(8,128)S(1)} %broadcast_select_fusion.5), kind=kOutput, calls=%fused_computation.17 | convolution fusion | flops 423106816 | bytes 20488192 | tf_op jit(solution)/shard_map/chqk,cqhd->ckhd/dot_general | solution.py:46
  475.9 6.6 copy.53
  482.5 6.8 copy.69
  489.3 9.1 copy.51
  498.4 7.2 copy.68
  505.6 10.1 %fusion.45 = f32[4096,896]{1,0:T(8,128)} fusion(bf16[4096,768]{0,1:T(8,128)(2,1)S(1)} %bitcast.116, bf16[896,768]{1,0:T(8,128)(2,1)S(1)} %copy-done), kind=kOutput, calls=%fused_computation.66 | convolution fusion | flops 5637144576 | bytes 22347776 | tf_op jit(solution)/shard_map/dot_general | solution.py:103
  515.7 12.1 %add_convert_fusion = bf16[4096,896]{1,0:T(8,128)(2,1)} fusion(f32[4096,896]{1,0:T(8,128)} %fusion.45, bf16[4096,768]{0,1:T(8,128)(2,1)S(1)} %bitcast.115, bf16[896,768]{1,0:T(8,128)(2,1)S(1)} %copy-done.10), kind=kOutput, calls=%fused_computation.4 | convolution fusion | flops 5644484608 | bytes 29687808 | tf_op jit(solution)/shard_map/dot_general | solution.py:104
  527.8 10.9 %copy.54 = bf16[896,32,128]{2,0,1:T(8,128)(2,1)} copy(bf16[896,32,128]{0,2,1:T(8,128)(2,1)} %bitcast.112) | data formatting | bytes 14680064 | tf_op jit(solution)/shard_map/reshape | solution.py:108
  538.8 8.7 broadcast_in_dim.93
  547.5 21.3 %scatter_fusion = bf16[896,64,128]{2,0,1:T(8,128)(2,1)} fusion(bf16[896,64,128]{2,0,1:T(8,128)(2,1)} %broadcast_in_dim.93, s32[32]{0:T(128)S(1)} %fusion.40, bf16[32,896,128]{2,1,0:T(8,128)(2,1)} %bitcast.108), kind=kCustom, calls=%fused_computation.2 | custom fusion | bytes 22020224 | tf_op jit(solution)/shard_map/scatter | solution.py:112
  568.8 16.6 %copy.55 = bf16[896,64,128]{2,1,0:T(8,128)(2,1)} copy(bf16[896,64,128]{2,0,1:T(8,128)(2,1)} %scatter_fusion) | data formatting | bytes 29360128 | tf_op jit(solution)/shard_map/scatter | solution.py:112
  585.5 22.3 %reshape.180 = bf16[4,224,8,1024]{3,2,1,0:T(8,128)(2,1)} reshape(bf16[896,64,128]{2,1,0:T(8,128)(2,1)} %copy.55) | data formatting | bytes 29360128 | tf_op jit(solution)/shard_map/reshape | solution.py:114
  607.8 16.7 %copy.56 = bf16[4,8,224,1024]{3,2,1,0:T(8,128)(2,1)} copy(bf16[4,8,224,1024]{3,1,2,0:T(8,128)(2,1)} %bitcast.106) | data formatting | bytes 29360128 | tf_op jit(solution)/shard_map/transpose | solution.py:114
  624.5 4.0 all-to-all-start.1
  628.5 7.4 fusion.24
  638.7 309.5 %all-to-all-done.1 = bf16[32,224,1024]{2,1,0:T(8,128)(2,1)} async-done(((bf16[32,224,1024]{2,1,0:T(8,128)(2,1)}), bf16[32,224,1024]{2,1,0:T(8,128)(2,1)}, u32[]{:S(2)}, u32[]{:S(2)}) %all-to-all-start.1) | async-done | bytes 14680096 | tf_op jit(solution)/shard_map/all_to_all | solution.py:116
  948.2 16.9 %copy.70 = f32[896,8,8,128]{3,2,1,0:T(8,128)} copy(bf16[896,8,8,128]{3,1,2,0:T(8,128)(2,1)} %bitcast.92) | data formatting | bytes 44040192
  965.1 14.1 %reduce_sum.29 = f32[8,224,8,128]{3,2,1,0:T(8,128)} reduce(f32[4,8,224,8,128]{4,3,2,1,0:T(8,128)} %bitcast.104, f32[]{:T(128)} %constant.57.clone.1), dimensions={0}, to_apply=%region_3.4 | reduce | flops 5505024 | bytes 36700164 | tf_op jit(solution)/shard_map/reduce_sum | solution.py:117
  979.2 5.5 bitcast_multiply_fusion
  984.8 4.0 copy.58
  (56 shorter events, 19.0 us)
Async XLA Ops:
  0.6 353.7 %copy-start = (bf16[896,768]{1,0:T(8,128)(2,1)S(1)}, bf16[896,768]{1,0:T(8,128)(2,1)}, u32[]{:S(2)}) copy-start(bf16[896,768]{1,0:T(8,128)(2,1)} %param.12) | copy-start | bytes 4128772
  3.0 0.6 copy-start.6
  17.4 8.3 copy-start.5
  17.4 327.3 %all-to-all-start = ((bf16[256,128,224]{1,2,0:T(8,128)(2,1)}), bf16[256,128,224]{1,2,0:T(8,128)(2,1)}, u32[]{:S(2)}, u32[]{:S(2)}) async-start(bf16[256,128,224]{1,2,0:T(8,128)(2,1)} %bitcast.107), calls=%async_computation | async-start | bytes 29360128 | tf_op jit(solution)/shard_map/all_to_all | solution.py:84
  25.0 6.9 copy-start.11
  25.0 6.9 copy-start.12
  354.3 14.8 %copy-start.2 = (bf16[32,4,128,224]{2,3,1,0:T(8,128)(2,1)S(1)}, bf16[32,4,128,224]{2,3,1,0:T(8,128)(2,1)}, u32[]{:S(2)}) copy-start(bf16[32,4,128,224]{2,3,1,0:T(8,128)(2,1)} %gather_fusion.1) | copy-start | bytes 22020100
  354.3 14.8 %copy-start.9 = (bf16[896,768]{1,0:T(8,128)(2,1)S(1)}, bf16[896,768]{1,0:T(8,128)(2,1)}, u32[]{:S(2)}) copy-start(bf16[896,768]{1,0:T(8,128)(2,1)} %param.13) | copy-start | bytes 4128772
  392.5 14.0 %copy-start.4 = (bf16[16,64,6,128]{3,2,1,0:T(8,128)(2,1)S(1)}, bf16[16,64,6,128]{3,2,1,0:T(8,128)(2,1)}, u32[]{:S(2)}) copy-start(bf16[16,64,6,128]{3,2,1,0:T(8,128)(2,1)} %broadcast_select_fusion.4) | copy-start | bytes 4718596
  406.5 8.5 copy-start.3
  421.7 0.6 copy-start.13
  498.4 17.3 %slice-start = ((s8[6291456]{0:T(1024)(128)(4,1)}), s8[4194304]{0:T(1024)(128)(4,1)S(1)}, s32[]{:S(2)}) async-start(s8[6291456]{0:T(1024)(128)(4,1)} %bitcast.113), calls=%async_computation.2 | async-start | bytes 8388608
  505.6 10.1 %slice-start.1 = ((s8[6291456]{0:T(1024)(128)(4,1)}), s8[2097152]{0:T(1024)(128)(4,1)S(1)}, s32[]{:S(2)}) async-start(s8[6291456]{0:T(1024)(128)(4,1)} %bitcast.113), calls=%async_computation.3 | async-start | bytes 4194304
  505.6 10.1 %copy-start.10 = (bf16[896,768]{1,0:T(8,128)(2,1)S(1)}, bf16[896,768]{1,0:T(8,128)(2,1)}, u32[]{:S(2)}) copy-start(bf16[896,768]{1,0:T(8,128)(2,1)} %param.13) | copy-start | bytes 4128772
  624.5 4.0 copy-start.14
  624.5 323.7 %all-to-all-start.1 = ((bf16[32,224,1024]{2,1,0:T(8,128)(2,1)}), bf16[32,224,1024]{2,1,0:T(8,128)(2,1)}, u32[]{:S(2)}, u32[]{:S(2)}) async-start(bf16[32,224,1024]{2,1,0:T(8,128)(2,1)} %bitcast.105), calls=%async_computation.1 | async-start | bytes 29360128 | tf_op jit(solution)/shard_map/all_to_all | solution.py:116
  965.1 14.1 %copy-start.7 = (f32[32,128]{1,0:T(8,128)S(1)}, f32[32,128]{1,0:T(8,128)}, u32[]{:S(2)}) copy-start(f32[32,128]{1,0:T(8,128)} %copy-done.6) | copy-start | bytes 49156
  965.1 14.1 %copy-start.8 = (s32[1,8,8]{2,1,0:T(8,128)S(1)}, s32[1,8,8]{2,1,0:T(8,128)}, u32[]{:S(2)}) copy-start(s32[1,8,8]{2,1,0:T(8,128)} %param.16) | copy-start | bytes 772
  979.2 9.5 copy-start.1
where the time goes:
time: 995 us; the launch traced here: 989 us
  waiting for transfers between devices  621 us (62%)
  local copies, waits for them, and re-layouts  205 us (21%)
  matrix products  129 us (13%)
  other arithmetic  21.1 us (2%)
  starting transfers between devices  11.6 us (1%)
    all_to_all x1, waiting for transfers between devices, per_device(): lax.all_to_all(spread, ('enc', 'span'), split_axis=0, concat_axis=0, tile...  311 us
    all_to_all x1, waiting for transfers between devices, per_device(): lax.all_to_all(grouped, ('enc', 'span'), split_axis=0, concat_axis=0, til...  310 us
    dot_general x1, matrix products, attend_blocks(): jnp.einsum('chqk,cqhd->ckhd', grad_scores, query_view, preferred_element_...  47.6 us
    scatter x2, local copies, waits for them, and re-layouts, per_device(): by_slot = jnp.zeros((enc_count * features, slot_total, NT), jnp.bfloat16)...  37.9 us
    unnamed x39, local copies, waits for them, and re-layouts  37.5 us
    reshape x1, local copies, waits for them, and re-layouts, per_device(): by_slot.reshape(enc_count, features, shard_count, capacity * NT)  22.3 us
  transfers between devices with their start and end apart: 2, of which 2 were waited for; matrix products, arithmetic and copies ran while one was open for 2% of the time, Pallas kernels for 0%

commit v1 on v0

v1 whole, which is shorter than its diff:
```python
import functools
import math

import jax
import jax.numpy as jnp
from jax import lax
from jax.experimental import pallas as pl
from jax.experimental.pallas import tpu as pltpu
from jax.sharding import PartitionSpec as P

HD = 128
CL = 64
NT = 128
NBR = 2
SPANS_PER_STEP = 2
VMEM_BYTES = 56 * 1024 * 1024

VMEM = pl.BlockSpec(memory_space=pltpu.VMEM)
SMEM = pl.BlockSpec(memory_space=pltpu.SMEM)


def params(**kw):
    return pltpu.CompilerParams(vmem_limit_bytes=VMEM_BYTES, **kw)


def pack_kernel(served_ref, store_ref, scale_ref, out_ref, encoded):
    blocks = store_ref.shape[0]

    def encode(b, carry):
        wide = store_ref[b].astype(jnp.float32)
        scaled = wide.T * scale_ref[pl.ds(b, 1), :]
        encoded[b] = scaled.astype(jnp.bfloat16)
        return carry

    lax.fori_loop(0, blocks, encode, 0)

    def copy(p, carry):
        out_ref[p] = encoded[served_ref[p]]
        return carry

    lax.fori_loop(0, out_ref.shape[0], copy, 0)


def pick_kernel(order_ref, in_ref, out_ref):
    def copy(i, carry):
        out_ref[i] = in_ref[order_ref[i]]
        return carry

    lax.fori_loop(0, out_ref.shape[0], copy, 0)


def attend_kernel(
    valid_ref,
    live_ref,
    x_ref,
    q_ref,
    c_ref,
    wkt_ref,
    wvt_ref,
    wk_ref,
    wv_ref,
    att_ref,
    part_ref,
    grad_k,
    grad_v,
):
    step = pl.program_id(0)
    heads = q_ref.shape[1] // HD
    enc, _, features, _ = x_ref.shape
    scale_factor = 1.0 / math.sqrt(HD)
    cols = lax.broadcasted_iota(jnp.int32, (1, NBR * NT), 1)
    dims_t = (((0,), (0,)), ((), ()))
    dims_nt = (((1,), (1,)), ((), ()))
    f32 = jnp.float32
    for j in range(SPANS_PER_STEP):
        span = step * SPANS_PER_STEP + j
        second = valid_ref[span].astype(f32)
        live = span < live_ref[0]
        mask = jnp.where(cols < NT, 1.0, second)
        halves = [x_ref[:, NBR * j + k].reshape(enc * features, NT) for k in range(NBR)]
        x = jnp.concatenate(halves, axis=1)
        key_t = jnp.dot(wkt_ref[...], x, preferred_element_type=f32).astype(jnp.bfloat16)
        value_t = jnp.dot(wvt_ref[...], x, preferred_element_type=f32).astype(jnp.bfloat16)
        rows = slice(j * CL, (j + 1) * CL)
        for h in range(heads):
            head = slice(h * HD, (h + 1) * HD)
            q = q_ref[rows, head]
            go = c_ref[rows, head]
            go = jnp.where(live, go, jnp.zeros_like(go))
            k_t = key_t[head, :]
            v_t = value_t[head, :]
            scores = jnp.dot(q, k_t, preferred_element_type=f32) * scale_factor
            weights = jnp.exp(scores) * mask
            probs = weights / jnp.sum(weights, axis=1, keepdims=True)
            low = probs.astype(jnp.bfloat16)
            mixture = lax.dot_general(low, v_t, dims_nt, preferred_element_type=f32)
            att_ref[rows, head] = jnp.where(live, mixture, 0.0).astype(jnp.bfloat16)
            grad_v[j, head, :] = lax.dot_general(
                go, low, dims_t, preferred_element_type=f32
            ).astype(jnp.bfloat16)
            grad_p = jnp.dot(go, v_t, preferred_element_type=f32)
            inner = jnp.sum(probs * grad_p, axis=1, keepdims=True)
            grad_s = (probs * (grad_p - inner) * scale_factor).astype(jnp.bfloat16)
            grad_k[j, head, :] = lax.dot_general(
                q, grad_s, dims_t, preferred_element_type=f32
            ).astype(jnp.bfloat16)
        part = jnp.dot(wk_ref[...], grad_k[j], preferred_element_type=f32)
        part = part + jnp.dot(wv_ref[...], grad_v[j], preferred_element_type=f32)
        part = part.astype(jnp.bfloat16)
        for k in range(NBR):
            half = part[:, k * NT : (k + 1) * NT]
            part_ref[:, NBR * j + k] = half.reshape(enc, features, NT)


def merge_kernel(order_ref, in_ref, out_ref):
    out_ref[...] = jnp.zeros_like(out_ref)

    def put(i, carry):
        total = in_ref[0, i].astype(jnp.float32)
        for e in range(1, in_ref.shape[0]):
            total = total + in_ref[e, i].astype(jnp.float32)
        out_ref[order_ref[i]] = total.astype(jnp.bfloat16)
        return carry

    lax.fori_loop(0, in_ref.shape[1], put, 0)


def gather_kernel(served_ref, in_ref, scale_ref, out_ref, total):
    total[...] = jnp.zeros_like(total)

    def add(p, carry):
        b = served_ref[p]
        total[b] = total[b] + in_ref[p].astype(jnp.float32)
        return carry

    lax.fori_loop(0, in_ref.shape[0], add, 0)

    def write(b, carry):
        scaled = total[b] * scale_ref[pl.ds(b, 1), :]
        out_ref[b] = scaled.T
        return carry

    lax.fori_loop(0, out_ref.shape[0], write, 0)


def per_device(
    queries,
    cotangent,
    key_weight,
    value_weight,
    neighbour_store,
    block_scale,
    fetch_index,
    neighbour_slot,
    second_valid,
    live_spans,
):
    enc_count = lax.axis_size("enc")
    shard_count = lax.axis_size("span")
    slot_total = shard_count * fetch_index.shape[2]
    blocks_here, _, features = neighbour_store.shape
    enc_features, head_width = key_weight.shape
    slot_order = neighbour_slot[0]
    used_count = slot_order.shape[0]
    spans = used_count // NBR
    served = fetch_index[0].reshape(slot_total)
    scale_wide = block_scale.astype(jnp.float32)
    bf16 = jnp.bfloat16

    outgoing = pl.pallas_call(
        pack_kernel,
        out_shape=jax.ShapeDtypeStruct((slot_total, features, NT), bf16),
        in_specs=[SMEM, VMEM, VMEM],
        out_specs=VMEM,
        scratch_shapes=[pltpu.VMEM((blocks_here, features, NT), bf16)],
        compiler_params=params(),
    )(served, neighbour_store, scale_wide)
    received = lax.all_to_all(outgoing, "span", split_axis=0, concat_axis=0, tiled=True)
    arranged = pl.pallas_call(
        pick_kernel,
        out_shape=jax.ShapeDtypeStruct((used_count, features, NT), bf16),
        in_specs=[SMEM, VMEM],
        out_specs=VMEM,
        compiler_params=params(),
    )(slot_order, received)
    whole = lax.all_gather(arranged, "enc", axis=0, tiled=False)

    step_blocks = SPANS_PER_STEP * NBR
    step_rows = SPANS_PER_STEP * CL
    resident = lambda i, *_: (0, 0)
    by_rows = pl.BlockSpec((step_rows, head_width), lambda i, *_: (i, 0))
    by_blocks = pl.BlockSpec((enc_count, step_blocks, features, NT), lambda i, *_: (0, i, 0, 0))
    attended, partial = pl.pallas_call(
        attend_kernel,
        out_shape=(
            jax.ShapeDtypeStruct(queries.shape, bf16),
            jax.ShapeDtypeStruct((enc_count, used_count, features, NT), bf16),
        ),
        grid_spec=pltpu.PrefetchScalarGridSpec(
            num_scalar_prefetch=2,
            grid=(spans // SPANS_PER_STEP,),
            in_specs=[
                by_blocks,
                by_rows,
                by_rows,
                pl.BlockSpec((head_width, enc_features), resident),
                pl.BlockSpec((head_width, enc_features), resident),
                pl.BlockSpec((enc_features, head_width), resident),
                pl.BlockSpec((enc_features, head_width), resident),
            ],
            out_specs=[by_rows, by_blocks],
            scratch_shapes=[
                pltpu.VMEM((SPANS_PER_STEP, head_width, NBR * NT), bf16),
                pltpu.VMEM((SPANS_PER_STEP, head_width, NBR * NT), bf16),
            ],
        ),
        compiler_params=params(dimension_semantics=("arbitrary",)),
    )(
        second_valid[0],
        live_spans,
        whole,
        queries,
        cotangent,
        key_weight.T,
        value_weight.T,
        key_weight,
        value_weight,
    )

    groups = lax.all_to_all(partial, "enc", split_axis=0, concat_axis=0, tiled=True)
    by_slot = pl.pallas_call(
        merge_kernel,
        out_shape=jax.ShapeDtypeStruct((slot_total, features, NT), bf16),
        in_specs=[SMEM, VMEM],
        out_specs=VMEM,
        compiler_params=params(),
    )(slot_order, groups)
    arrived = lax.all_to_all(by_slot, "span", split_axis=0, concat_axis=0, tiled=True)
    grad_store = pl.pallas_call(
        gather_kernel,
        out_shape=jax.ShapeDtypeStruct(neighbour_store.shape, jnp.float32),
        in_specs=[SMEM, VMEM, VMEM],
        out_specs=VMEM,
        scratch_shapes=[pltpu.VMEM((blocks_here, features, NT), jnp.float32)],
        compiler_params=params(),
    )(served, arrived, scale_wide)
    return (attended, grad_store)


def solution(mesh):
    return jax.shard_map(
        per_device,
        mesh=mesh,
        in_specs=(
            P("span", "enc"),
            P("span", "enc"),
            P(None, "enc"),
            P(None, "enc"),
            P("span", None, "enc"),
            P("span", None),
            P("span", None, None),
            P("span", None),
            P("span", None),
            P("span"),
        ),
        out_specs=(P("span", "enc"), P("span", None, "enc")),
        check_vma=False,
    )
```

time: 995 us -> 456 us (0.46)
  waiting for transfers between devices: 621 us -> 73.5 us
  blocking collectives: 0 us -> 266 us
  local copies, waits for them, and re-layouts: 205 us -> 14.4 us
  matrix products: 129 us -> 0 us
  Pallas kernels: 0 us -> 85.6 us
  other arithmetic: 21.1 us -> 1.29 us
  between operations: 1.81 us -> 14.8 us
  starting transfers between devices: 11.6 us -> 0.04 us
    all_to_all x2 -> x0, waiting for transfers between devices: 621 us -> none  [the longest x1 311 us: per_device(): lax.all_to_all(spread, ('enc', 'span'), split_axis=0, concat_axis=0, tile...]
    all_to_all x0 -> x3, blocking collectives: none -> 266 us  [the longest x1 89.2 us: per_device(): lax.all_to_all(outgoing, 'span', split_axis=0, concat_axis=0, tiled=True)]
    dot_general x10 -> x0, matrix products: 129 us -> none  [the longest x1 47.6 us: attend_blocks(): jnp.einsum('chqk,cqhd->ckhd', grad_scores, query_view, preferred_element_...]
    pallas_call x0 -> x5, Pallas kernels: none -> 85.6 us  [the longest x1 59.8 us: per_device(): pl.pallas_call(attend_kernel, out_shape=(jax.ShapeDtypeStruct(queries.sha...]
    all_gather x0 -> x1, waiting for transfers between devices: none -> 73.4 us  [per_device(): whole = lax.all_gather(arranged, 'enc', axis=0, tiled=False)]
    reshape x4 -> x0, local copies, waits for them, and re-layouts: 39.4 us -> none  [the longest x1 22.3 us: per_device(): by_slot.reshape(enc_count, features, shard_count, capacity * NT)]
    scatter x2 -> x0, local copies, waits for them, and re-layouts: 37.9 us -> none  [per_device(): by_slot = jnp.zeros((enc_count * features, slot_total, NT), jnp.bfloat16)...]
    another operation x2 -> x0, local copies, waits for them, and re-layouts: 27.6 us -> none  [the longest x1 14 us: attend_blocks(): keys_view = key_proj.reshape(spans, NBR * NT, heads_here, HD)]
  transfers between devices with their start and end apart: 2 -> 1, of which waited for: 2 -> 1; matrix products, arithmetic and copies ran while one was open for 2% -> 1% of each run, Pallas kernels for 0% -> 0%
where the time goes in v1:
time: 456 us; the launch traced here: 455 us
  blocking collectives  266 us (58%)
  Pallas kernels  85.6 us (19%)
  waiting for transfers between devices  73.5 us (16%)
  between operations  14.8 us (3%)
  local copies, waits for them, and re-layouts  14.4 us (3%)
    all_to_all x1, blocking collectives, per_device(): lax.all_to_all(outgoing, 'span', split_axis=0, concat_axis=0, tiled=True)  89.2 us
    all_to_all x1, blocking collectives, per_device(): lax.all_to_all(partial, 'enc', split_axis=0, concat_axis=0, tiled=True)  89.1 us
    all_to_all x1, blocking collectives, per_device(): lax.all_to_all(by_slot, 'span', split_axis=0, concat_axis=0, tiled=True)  87.5 us
    all_gather x1, waiting for transfers between devices, per_device(): whole = lax.all_gather(arranged, 'enc', axis=0, tiled=False)  73.4 us
    pallas_call x1, Pallas kernels, per_device(): pl.pallas_call(attend_kernel, out_shape=(jax.ShapeDtypeStruct(queries.sha...  59.8 us
    unnamed x8, local copies, waits for them, and re-layouts  13.1 us
  transfers between devices with their start and end apart: 1, of which 1 were waited for; matrix products, arithmetic and copies ran while one was open for 1% of the time, Pallas kernels for 0%

profile of v1, /device:TPU:0, one launch (start us, length us, event | category | flops | bytes accessed | tf_op | source)
XLA Modules:
  0.0 455.5 jit_solution(13029916552358902980)
XLA Ops:
  7.2 0.0 all-gather.3.cloned.1.call-start
  7.2 1.3 reshape_squeeze.3.served_ref
  8.5 1.3 convert_element_type.3.scale_ref
  9.8 3.9 copy.16.store_ref
  13.8 7.3 %shard_map.113 = bf16[64,224,128]{2,1,0:T(8,128)(2,1)} custom-call(s32[64]{0:T(128)} %reshape_squeeze.3.served_ref, bf16[32,128,224]{2,1,0:T(8,128)(2,1)} %copy.16.store_ref, f32[32,128]{1,0:T(8,128)} %convert_element_type.3.scale_ref), custom_call_target="tpu_custom_call" | custom-call | tf_op jit(solution)/shard_map/pallas_call | solution.py:170
  21.1 89.2 %all_to_all.15.in_ref = bf16[64,224,128]{2,1,0:T(8,128)(2,1)} all-to-all(bf16[64,224,128]{2,1,0:T(8,128)(2,1)} %shard_map.113), channel_id=1, replica_groups=mesh['enc'=4,'span'=8] {'span'}, dimensions={0} | all-to-all | bytes 7340032 | tf_op jit(solution)/shard_map/all_to_all | solution.py:178
  110.3 3.6 shard_map.114
  113.9 0.0 copy-start
  113.9 0.0 copy-start.1
  113.9 0.0 all-gather.3.cloned.1.call-update
  114.7 0.5 copy-done
  115.2 1.6 copy.17
  116.8 0.0 copy-done.1
  116.8 1.6 copy.18
  118.4 73.4 %all-gather.3.cloned.1.call-done = bf16[128,224,128]{2,1,0:T(8,128)(2,1)} async-done(((bf16[32,224,128]{2,1,0:T(8,128)(2,1)}), bf16[128,224,128]{2,1,0:T(8,128)(2,1)}) %all-gather.3.cloned.1.call-update) | async-done | bytes 7340048 | tf_op jit(solution)/shard_map/all_gather | solution.py:186
  191.8 59.8 %shard_map.115 = (bf16[1024,768]{1,0:T(8,128)(2,1)}, bf16[4,32,224,128]{3,2,1,0:T(8,128)(2,1)}) custom-call(s32[16]{0:T(128)} %bitcast.10, s32[1]{0:T(128)S(6)} %copy.20.live_ref, bf16[4,32,224,128]{3,2,1,0:T(8,128)(2,1)} %bitcast.5, bf16[1024,768]{1,0:T(8,128)(2,1)} %q_ref.1, bf16[1024,768]{1,0:T(8,128)(2,1)} %c_ref.1, bf16[768,896]{1,0:T(8,128)(2,1)} %bitcast.6, ...), custom_call_target="tpu_custom_call" | custom-call | tf_op jit(solution)/shard_map/pallas_call | solution.py:193
  251.7 89.1 %all_to_all.16.in_ref = bf16[4,32,224,128]{3,2,1,0:T(8,128)(2,1)} all-to-all(bf16[4,32,224,128]{3,2,1,0:T(8,128)(2,1)} %get-tuple-element.5), channel_id=1, replica_groups=mesh['enc'=4,'span'=8] {'enc'}, dimensions={0} | all-to-all | bytes 14680064 | tf_op jit(solution)/shard_map/all_to_all | solution.py:230
  340.8 6.5 %shard_map.116 = bf16[64,224,128]{2,1,0:T(8,128)(2,1)} custom-call(s32[32]{0:T(128)} %bitcast.9, bf16[4,32,224,128]{3,2,1,0:T(8,128)(2,1)} %all_to_all.16.in_ref), custom_call_target="tpu_custom_call" | custom-call | tf_op jit(solution)/shard_map/pallas_call | solution.py:231
  347.3 87.5 %all_to_all.17.in_ref = bf16[64,224,128]{2,1,0:T(8,128)(2,1)} all-to-all(bf16[64,224,128]{2,1,0:T(8,128)(2,1)} %shard_map.116), channel_id=1, replica_groups=mesh['enc'=4,'span'=8] {'span'}, dimensions={0} | all-to-all | bytes 7340032 | tf_op jit(solution)/shard_map/all_to_all | solution.py:238
  434.8 8.4 %shard_map.117 = f32[32,128,224]{2,1,0:T(8,128)} custom-call(s32[64]{0:T(128)} %reshape_squeeze.3.served_ref, bf16[64,224,128]{2,1,0:T(8,128)(2,1)} %all_to_all.17.in_ref, f32[32,128]{1,0:T(8,128)} %convert_element_type.3.scale_ref), custom_call_target="tpu_custom_call" | custom-call | tf_op jit(solution)/shard_map/pallas_call | solution.py:239
  443.2 5.5 %copy.19 = f32[32,128,224]{1,2,0:T(8,128)} copy(f32[32,128,224]{2,1,0:T(8,128)} %shard_map.117) | data formatting | bytes 7340032
Async XLA Ops:
  7.2 184.7 %all-gather.3.cloned.1.call-start = ((), (), s32[]{:S(2)}) async-start(), calls=%async_computation.3 | async-start | bytes 9175040 | tf_op jit(solution)/shard_map/all_gather | solution.py:186
  113.9 1.4 copy-start
  113.9 2.9 copy-start.1
Sparse Core Ops, SparseCore 0:
  114.0 77.7 all-gather.2

commit v2 on v1

--- a/solution.py
+++ b/solution.py
@@ -13,10 +13,13 @@
 NT = 128
 NBR = 2
 SPANS_PER_STEP = 2
+CHUNKS = 7
+MESH = pl.DeviceIdType.MESH
 VMEM_BYTES = 56 * 1024 * 1024
 
 VMEM = pl.BlockSpec(memory_space=pltpu.VMEM)
 SMEM = pl.BlockSpec(memory_space=pltpu.SMEM)
+ANY = pl.BlockSpec(memory_space=pl.ANY)
 
 
 def params(**kw):
@@ -34,19 +37,169 @@
 
     lax.fori_loop(0, blocks, encode, 0)
 
+    chunks, slots, rows, _ = out_ref.shape
+
     def copy(p, carry):
-        out_ref[p] = encoded[served_ref[p]]
-        return carry
-
-    lax.fori_loop(0, out_ref.shape[0], copy, 0)
-
-
-def pick_kernel(order_ref, in_ref, out_ref):
-    def copy(i, carry):
-        out_ref[i] = in_ref[order_ref[i]]
-        return carry
-
-    lax.fori_loop(0, out_ref.shape[0], copy, 0)
+        b = served_ref[p]
+        for c in range(chunks):
+            out_ref[c, p] = encoded[b, c * rows : (c + 1) * rows]
+        return carry
+
+    lax.fori_loop(0, slots, copy, 0)
+
+
+def greet(me_enc, me_span, enc_count, shard_count):
+    barrier = pltpu.get_barrier_semaphore()
+
+    def greet_span(d, carry):
+        peer = lax.rem(me_span + d, shard_count)
+        pl.semaphore_signal(barrier, inc=1, device_id=(me_enc, peer), device_id_type=MESH)
+        return carry
+
+    def greet_enc(d, carry):
+        peer = lax.rem(me_enc + d, enc_count)
+        pl.semaphore_signal(barrier, inc=1, device_id=(peer, me_span), device_id_type=MESH)
+        return carry
+
+    lax.fori_loop(1, shard_count, greet_span, 0)
+    lax.fori_loop(1, enc_count, greet_enc, 0)
+    pl.semaphore_wait(barrier, shard_count + enc_count - 2)
+
+
+def each(count, act):
+    def body(d, carry):
+        act(d)
+        return carry
+
+    lax.fori_loop(1, count, body, 0)
+
+
+def fetch_kernel(enc_count, shard_count, order_ref, in_ref, out_ref, *scratch):
+    chunks, slots, _, _ = in_ref.shape
+    capacity = slots // shard_count
+    used = order_ref.shape[0]
+    received, mine = scratch[:chunks], scratch[chunks : 2 * chunks]
+    span_send, span_recv, span_own, enc_send, enc_recv, enc_own = scratch[2 * chunks :]
+    me_enc, me_span = lax.axis_index("enc"), lax.axis_index("span")
+
+    def span_copy(c, d):
+        peer = lax.rem(me_span + d, shard_count)
+        return pltpu.make_async_remote_copy(
+            src_ref=in_ref.at[c, pl.ds(peer * capacity, capacity)],
+            dst_ref=received[c].at[pl.ds(me_span * capacity, capacity)],
+            send_sem=span_send.at[c, d],
+            recv_sem=span_recv.at[c, d],
+            device_id=(me_enc, peer),
+            device_id_type=MESH,
+        )
+
+    def span_local(c):
+        here = pl.ds(me_span * capacity, capacity)
+        return pltpu.make_async_copy(in_ref.at[c, here], received[c].at[here], span_own.at[c])
+
+    def enc_copy(c, d):
+        peer = lax.rem(me_enc + d, enc_count)
+        return pltpu.make_async_remote_copy(
+            src_ref=mine[c],
+            dst_ref=out_ref.at[c, me_enc],
+            send_sem=enc_send.at[c, d],
+            recv_sem=enc_recv.at[c, d],
+            device_id=(peer, me_span),
+            device_id_type=MESH,
+        )
+
+    def enc_local(c):
+        return pltpu.make_async_copy(mine[c], out_ref.at[c, me_enc], enc_own.at[c])
+
+    greet(me_enc, me_span, enc_count, shard_count)
+    for c in range(chunks):
+        each(shard_count, lambda d: span_copy(c, d).start())
+        span_local(c).start()
+    for c in range(chunks):
+        each(shard_count, lambda d: span_copy(c, d).wait_recv())
+        span_local(c).wait()
+
+        def pick(i, carry):
+            mine[c][i] = received[c][order_ref[i]]
+            return carry
+
+        lax.fori_loop(0, used, pick, 0)
+        each(enc_count, lambda d: enc_copy(c, d).start())
+        enc_local(c).start()
+    for c in range(chunks):
+        each(shard_count, lambda d: span_copy(c, d).wait_send())
+        each(enc_count, lambda d: enc_copy(c, d).wait())
+        enc_local(c).wait()
+
+
+def return_kernel(enc_count, shard_count, place_ref, in_ref, out_ref, *scratch):
+    chunks, _, used, _, _ = in_ref.shape
+    slots = out_ref.shape[1]
+    capacity = slots // shard_count
+    groups = scratch[:chunks]
+    merged = scratch[chunks : 2 * chunks]
+    by_slot = scratch[2 * chunks : 3 * chunks]
+    span_send, span_recv, span_own, enc_send, enc_recv, enc_own = scratch[3 * chunks :]
+    me_enc, me_span = lax.axis_index("enc"), lax.axis_index("span")
+
+    def enc_copy(c, d):
+        peer = lax.rem(me_enc + d, enc_count)
+        return pltpu.make_async_remote_copy(
+            src_ref=in_ref.at[c, peer],
+            dst_ref=groups[c].at[me_enc],
+            send_sem=enc_send.at[c, d],
+            recv_sem=enc_recv.at[c, d],
+            device_id=(peer, me_span),
+            device_id_type=MESH,
+        )
+
+    def enc_local(c):
+        return pltpu.make_async_copy(in_ref.at[c, me_enc], groups[c].at[me_enc], enc_own.at[c])
+
+    def span_copy(c, d):
+        peer = lax.rem(me_span + d, shard_count)
+        return pltpu.make_async_remote_copy(
+            src_ref=by_slot[c].at[pl.ds(peer * capacity, capacity)],
+            dst_ref=out_ref.at[c, pl.ds(me_span * capacity, capacity)],
+            send_sem=span_send.at[c, d],
+            recv_sem=span_recv.at[c, d],
+            device_id=(me_enc, peer),
+            device_id_type=MESH,
+        )
+
+    def span_local(c):
+        here = pl.ds(me_span * capacity, capacity)
+        return pltpu.make_async_copy(by_slot[c].at[here], out_ref.at[c, here], span_own.at[c])
+
+    greet(me_enc, me_span, enc_count, shard_count)
+    for c in range(chunks):
+        each(enc_count, lambda d: enc_copy(c, d).start())
+        enc_local(c).start()
+    for c in range(chunks):
+        each(enc_count, lambda d: enc_copy(c, d).wait_recv())
+        enc_local(c).wait()
+        merged[c][used] = jnp.zeros(merged[c].shape[1:], jnp.bfloat16)
+
+        def add(i, carry):
+            total = groups[c][0, i].astype(jnp.float32)
+            for e in range(1, enc_count):
+                total = total + groups[c][e, i].astype(jnp.float32)
+            merged[c][i] = total.astype(jnp.bfloat16)
+            return carry
+
+        lax.fori_loop(0, used, add, 0)
+
+        def put(p, carry):
+            by_slot[c][p] = merged[c][place_ref[p]]
+            return carry
+
+        lax.fori_loop(0, slots, put, 0)
+        each(shard_count, lambda d: span_copy(c, d).start())
+        span_local(c).start()
+    for c in range(chunks):
+        each(enc_count, lambda d: enc_copy(c, d).wait_send())
+        each(shard_count, lambda d: span_copy(c, d).wait())
+        span_local(c).wait()
 
 
 def attend_kernel(
@@ -66,7 +219,8 @@
 ):
     step = pl.program_id(0)
     heads = q_ref.shape[1] // HD
-    enc, _, features, _ = x_ref.shape
+    chunks, enc, _, rows_c, _ = x_ref.shape
+    pieces = [(e, c) for e in range(enc) for c in range(chunks)]
     scale_factor = 1.0 / math.sqrt(HD)
     cols = lax.broadcasted_iota(jnp.int32, (1, NBR * NT), 1)
     dims_t = (((0,), (0,)), ((), ()))
@@ -77,7 +231,10 @@
         second = valid_ref[span].astype(f32)
         live = span < live_ref[0]
         mask = jnp.where(cols < NT, 1.0, second)
-        halves = [x_ref[:, NBR * j + k].reshape(enc * features, NT) for k in range(NBR)]
+        halves = [
+            jnp.concatenate([x_ref[c, e, NBR * j + k] for e, c in pieces], axis=0)
+            for k in range(NBR)
+        ]
         x = jnp.concatenate(halves, axis=1)
         key_t = jnp.dot(wkt_ref[...], x, preferred_element_type=f32).astype(jnp.bfloat16)
         value_t = jnp.dot(wvt_ref[...], x, preferred_element_type=f32).astype(jnp.bfloat16)
@@ -108,32 +265,24 @@
         part = part + jnp.dot(wv_ref[...], grad_v[j], preferred_element_type=f32)
         part = part.astype(jnp.bfloat16)
         for k in range(NBR):
-            half = part[:, k * NT : (k + 1) * NT]
-            part_ref[:, NBR * j + k] = half.reshape(enc, features, NT)
-
-
-def merge_kernel(order_ref, in_ref, out_ref):
-    out_ref[...] = jnp.zeros_like(out_ref)
-
-    def put(i, carry):
-        total = in_ref[0, i].astype(jnp.float32)
-        for e in range(1, in_ref.shape[0]):
-            total = total + in_ref[e, i].astype(jnp.float32)
-        out_ref[order_ref[i]] = total.astype(jnp.bfloat16)
-        return carry
-
-    lax.fori_loop(0, in_ref.shape[1], put, 0)
+            for n, (e, c) in enumerate(pieces):
+                part_ref[c, e, NBR * j + k] = part[
+                    n * rows_c : (n + 1) * rows_c, k * NT : (k + 1) * NT
+                ]
 
 
 def gather_kernel(served_ref, in_ref, scale_ref, out_ref, total):
+    chunks, slots, rows, _ = in_ref.shape
     total[...] = jnp.zeros_like(total)
 
     def add(p, carry):
         b = served_ref[p]
-        total[b] = total[b] + in_ref[p].astype(jnp.float32)
-        return carry
-
-    lax.fori_loop(0, in_ref.shape[0], add, 0)
+        for c in range(chunks):
+            here = slice(c * rows, (c + 1) * rows)
+            total[b, here] = total[b, here] + in_ref[c, p].astype(jnp.float32)
+        return carry
+
+    lax.fori_loop(0, slots, add, 0)
 
     def write(b, carry):
         scaled = total[b] * scale_ref[pl.ds(b, 1), :]
@@ -166,35 +315,52 @@
     served = fetch_index[0].reshape(slot_total)
     scale_wide = block_scale.astype(jnp.float32)
     bf16 = jnp.bfloat16
+    rows = features // CHUNKS
+    used_index = jnp.arange(used_count, dtype=jnp.int32)
+    slot_index = jnp.arange(slot_total, dtype=jnp.int32)
+    named = slot_order[None, :] == slot_index[:, None]
+    place = jnp.min(jnp.where(named, used_index[None, :], used_count), axis=1)
 
     outgoing = pl.pallas_call(
         pack_kernel,
-        out_shape=jax.ShapeDtypeStruct((slot_total, features, NT), bf16),
+        out_shape=jax.ShapeDtypeStruct((CHUNKS, slot_total, rows, NT), bf16),
         in_specs=[SMEM, VMEM, VMEM],
         out_specs=VMEM,
         scratch_shapes=[pltpu.VMEM((blocks_here, features, NT), bf16)],
         compiler_params=params(),
     )(served, neighbour_store, scale_wide)
-    received = lax.all_to_all(outgoing, "span", split_axis=0, concat_axis=0, tiled=True)
-    arranged = pl.pallas_call(
-        pick_kernel,
-        out_shape=jax.ShapeDtypeStruct((used_count, features, NT), bf16),
+    dma = pltpu.SemaphoreType.DMA
+    semaphores = [
+        dma((CHUNKS, shard_count)),
+        dma((CHUNKS, shard_count)),
+        dma((CHUNKS,)),
+        dma((CHUNKS, enc_count)),
+        dma((CHUNKS, enc_count)),
+        dma((CHUNKS,)),
+    ]
+    whole = pl.pallas_call(
+        functools.partial(fetch_kernel, enc_count, shard_count),
+        out_shape=jax.ShapeDtypeStruct((CHUNKS, enc_count, used_count, rows, NT), bf16),
         in_specs=[SMEM, VMEM],
-        out_specs=VMEM,
-        compiler_params=params(),
-    )(slot_order, received)
-    whole = lax.all_gather(arranged, "enc", axis=0, tiled=False)
+        out_specs=ANY,
+        scratch_shapes=[pltpu.VMEM((slot_total, rows, NT), bf16)] * CHUNKS
+        + [pltpu.VMEM((used_count, rows, NT), bf16)] * CHUNKS
+        + semaphores,
+        compiler_params=params(collective_id=0, has_side_effects=True),
+    )(slot_order, outgoing)
 
     step_blocks = SPANS_PER_STEP * NBR
     step_rows = SPANS_PER_STEP * CL
     resident = lambda i, *_: (0, 0)
     by_rows = pl.BlockSpec((step_rows, head_width), lambda i, *_: (i, 0))
-    by_blocks = pl.BlockSpec((enc_count, step_blocks, features, NT), lambda i, *_: (0, i, 0, 0))
+    by_blocks = pl.BlockSpec(
+        (CHUNKS, enc_count, step_blocks, rows, NT), lambda i, *_: (0, 0, i, 0, 0)
+    )
     attended, partial = pl.pallas_call(
         attend_kernel,
         out_shape=(
             jax.ShapeDtypeStruct(queries.shape, bf16),
-            jax.ShapeDtypeStruct((enc_count, used_count, features, NT), bf16),
+            jax.ShapeDtypeStruct(whole.shape, bf16),
         ),
         grid_spec=pltpu.PrefetchScalarGridSpec(
             num_scalar_prefetch=2,
@@ -227,15 +393,17 @@
         value_weight,
     )
 
-    groups = lax.all_to_all(partial, "enc", split_axis=0, concat_axis=0, tiled=True)
-    by_slot = pl.pallas_call(
-        merge_kernel,
-        out_shape=jax.ShapeDtypeStruct((slot_total, features, NT), bf16),
-        in_specs=[SMEM, VMEM],
-        out_specs=VMEM,
-        compiler_params=params(),
-    )(slot_order, groups)
-    arrived = lax.all_to_all(by_slot, "span", split_axis=0, concat_axis=0, tiled=True)
+    arrived = pl.pallas_call(
+        functools.partial(return_kernel, enc_count, shard_count),
+        out_shape=jax.ShapeDtypeStruct((CHUNKS, slot_total, rows, NT), bf16),
+        in_specs=[SMEM, ANY],
+        out_specs=ANY,
+        scratch_shapes=[pltpu.VMEM((enc_count, used_count, rows, NT), bf16)] * CHUNKS
+        + [pltpu.VMEM((used_count + 1, rows, NT), bf16)] * CHUNKS
+        + [pltpu.VMEM((slot_total, rows, NT), bf16)] * CHUNKS
+        + semaphores,
+        compiler_params=params(collective_id=1, has_side_effects=True),
+    )(place, partial)
     grad_store = pl.pallas_call(
         gather_kernel,
         out_shape=jax.ShapeDtypeStruct(neighbour_store.shape, jnp.float32),

time: 456 us -> 310 us (0.68)
  blocking collectives: 266 us -> 0 us
  Pallas kernels: 85.6 us -> 291 us
  waiting for transfers between devices: 73.5 us -> 0 us
  between operations: 14.8 us -> 1.33 us
    all_to_all x3 -> x0, blocking collectives: 266 us -> none  [the longest x1 89.2 us: per_device(): lax.all_to_all(outgoing, 'span', split_axis=0, concat_axis=0, tiled=True)]
    pallas_call x3, Pallas kernels: 17.4 us -> 223 us  [the longest x1 117 us: per_device(): pl.pallas_call(functools.partial(fetch_kernel, enc_count, shard_count), o...]
    all_gather x1 -> x0, waiting for transfers between devices: 73.4 us -> none  [per_device(): whole = lax.all_gather(arranged, 'enc', axis=0, tiled=False)]
    unnamed x8 -> x10, local copies, waits for them, and re-layouts: 13.1 us -> 12.6 us
  transfers between devices with their start and end apart: 1 -> 0, of which waited for: 1 -> 0; matrix products, arithmetic and copies ran while one was open for 1% -> 0% of each run, Pallas kernels for 0% -> 0%
where the time goes in v2:
time: 310 us; the launch traced here: 309 us
  Pallas kernels  291 us (94%)
  local copies, waits for them, and re-layouts  13.9 us (4%)
    pallas_call x1, Pallas kernels, per_device(): pl.pallas_call(functools.partial(fetch_kernel, enc_count, shard_count), o...  117 us
    pallas_call x1, Pallas kernels, per_device(): pl.pallas_call(functools.partial(return_kernel, enc_count, shard_count),...  99.2 us
    pallas_call x1, Pallas kernels, per_device(): pl.pallas_call(attend_kernel, out_shape=(jax.ShapeDtypeStruct(queries.sha...  59.8 us
    unnamed x10, local copies, waits for them, and re-layouts  12.6 us
    pallas_call x1, Pallas kernels, per_device(): pl.pallas_call(gather_kernel, out_shape=jax.ShapeDtypeStruct(neighbour_st...  8.42 us
    pallas_call x1, Pallas kernels, per_device(): pl.pallas_call(pack_kernel, out_shape=jax.ShapeDtypeStruct((CHUNKS, slot_...  7.32 us

profile of v2, /device:TPU:0, one launch (start us, length us, event | category | flops | bytes accessed | tf_op | source)
XLA Modules:
  0.0 308.5 jit_solution(6402300169865421203)
XLA Ops:
  0.6 1.3 convert_element_type.3.scale_ref
  1.9 1.3 reshape_squeeze.3.served_ref
  3.3 4.0 %copy.16.store_ref = bf16[32,128,224]{2,1,0:T(8,128)(2,1)} copy(bf16[32,128,224]{1,2,0:T(8,128)(2,1)} %param.14) | data formatting | bytes 3670016 | tf_op args[4]
  7.2 7.3 %shard_map.113.in_ref = bf16[7,64,32,128]{3,2,1,0:T(8,128)(2,1)} custom-call(s32[64]{0:T(128)} %reshape_squeeze.3.served_ref, bf16[32,128,224]{2,1,0:T(8,128)(2,1)} %copy.16.store_ref, f32[32,128]{1,0:T(8,128)} %convert_element_type.3.scale_ref), custom_call_target="tpu_custom_call" | custom-call | tf_op jit(solution)/shard_map/pallas_call | solution.py:324
  14.5 0.0 copy-start
  14.5 116.6 %shard_map.114.x_ref = bf16[7,4,32,32,128]{4,3,2,1,0:T(8,128)(2,1)} custom-call(s32[32]{0:T(128)} %bitcast.7, bf16[7,64,32,128]{3,2,1,0:T(8,128)(2,1)} %shard_map.113.in_ref), custom_call_target="tpu_custom_call" | custom-call | tf_op jit(solution)/shard_map/pallas_call | solution.py:341
  131.2 0.0 copy-done
  131.2 0.0 copy-start.1
  131.2 1.6 copy.17
  132.8 0.0 copy-done.1
  132.8 1.6 copy.18
  135.0 0.0 copy-start.2
  135.0 59.8 %shard_map.115 = (bf16[1024,768]{1,0:T(8,128)(2,1)}, bf16[7,4,32,32,128]{4,3,2,1,0:T(8,128)(2,1)}) custom-call(s32[16]{0:T(128)} %bitcast.6, s32[1]{0:T(128)S(6)} %copy.20.live_ref, bf16[7,4,32,32,128]{4,3,2,1,0:T(8,128)(2,1)} %shard_map.114.x_ref, bf16[1024,768]{1,0:T(8,128)(2,1)} %q_ref.1, bf16[1024,768]{1,0:T(8,128)(2,1)} %c_ref.1, ...), custom_call_target="tpu_custom_call" | custom-call | tf_op jit(solution)/shard_map/pallas_call | solution.py:359
  194.8 0.0 copy-done.2
  194.8 0.6 select_reduce_fusion.place_ref
  195.4 99.2 %shard_map.116.in_ref = bf16[7,64,32,128]{3,2,1,0:T(8,128)(2,1)} custom-call(s32[64]{0:T(128)} %select_reduce_fusion.place_ref, bf16[7,4,32,32,128]{4,3,2,1,0:T(8,128)(2,1)} %get-tuple-element.5.in_ref), custom_call_target="tpu_custom_call" | custom-call | tf_op jit(solution)/shard_map/pallas_call | solution.py:396
  294.6 8.4 %shard_map.117 = f32[32,128,224]{2,1,0:T(8,128)} custom-call(s32[64]{0:T(128)} %reshape_squeeze.3.served_ref, bf16[7,64,32,128]{3,2,1,0:T(8,128)(2,1)} %shard_map.116.in_ref, f32[32,128]{1,0:T(8,128)} %convert_element_type.3.scale_ref), custom_call_target="tpu_custom_call" | custom-call | tf_op jit(solution)/shard_map/pallas_call | solution.py:407
  303.0 5.5 %copy.19 = f32[32,128,224]{1,2,0:T(8,128)} copy(f32[32,128,224]{2,1,0:T(8,128)} %shard_map.117) | data formatting | bytes 7340032
Async XLA Ops:
  14.5 116.6 %copy-start = (bf16[896,768]{1,0:T(8,128)(2,1)S(1)}, bf16[896,768]{1,0:T(8,128)(2,1)}, u32[]{:S(2)}) copy-start(bf16[896,768]{1,0:T(8,128)(2,1)} %wk_ref.1) | copy-start | bytes 4128772
  131.2 1.6 copy-start.1
  135.0 59.8 %copy-start.2 = (s32[1,32]{1,0:T(1,128)S(1)}, s32[1,32]{1,0:T(1,128)}, u32[]{:S(2)}) copy-start(s32[1,32]{1,0:T(1,128)} %param.17) | copy-start | bytes 388

commit v3 on v2

--- a/solution.py
+++ b/solution.py
@@ -13,7 +13,9 @@
 NT = 128
 NBR = 2
 SPANS_PER_STEP = 2
+SPANS_TOGETHER = 1
 CHUNKS = 7
+WINDOW = 1
 MESH = pl.DeviceIdType.MESH
 VMEM_BYTES = 56 * 1024 * 1024
 
@@ -24,28 +26,6 @@
 
 def params(**kw):
     return pltpu.CompilerParams(vmem_limit_bytes=VMEM_BYTES, **kw)
-
-
-def pack_kernel(served_ref, store_ref, scale_ref, out_ref, encoded):
-    blocks = store_ref.shape[0]
-
-    def encode(b, carry):
-        wide = store_ref[b].astype(jnp.float32)
-        scaled = wide.T * scale_ref[pl.ds(b, 1), :]
-        encoded[b] = scaled.astype(jnp.bfloat16)
-        return carry
-
-    lax.fori_loop(0, blocks, encode, 0)
-
-    chunks, slots, rows, _ = out_ref.shape
-
-    def copy(p, carry):
-        b = served_ref[p]
-        for c in range(chunks):
-            out_ref[c, p] = encoded[b, c * rows : (c + 1) * rows]
-        return carry
-
-    lax.fori_loop(0, slots, copy, 0)
 
 
 def greet(me_enc, me_span, enc_count, shard_count):
@@ -74,18 +54,21 @@
     lax.fori_loop(1, count, body, 0)
 
 
-def fetch_kernel(enc_count, shard_count, order_ref, in_ref, out_ref, *scratch):
-    chunks, slots, _, _ = in_ref.shape
+def fetch_kernel(
+    enc_count, shard_count, order_ref, served_ref, store_ref, scale_ref, out_ref, *scratch
+):
+    chunks, _, used, rows, _ = out_ref.shape
+    slots = served_ref.shape[0]
     capacity = slots // shard_count
-    used = order_ref.shape[0]
-    received, mine = scratch[:chunks], scratch[chunks : 2 * chunks]
-    span_send, span_recv, span_own, enc_send, enc_recv, enc_own = scratch[2 * chunks :]
+    outgoing, received = scratch[:chunks], scratch[chunks : 2 * chunks]
+    mine = scratch[2 * chunks : 3 * chunks]
+    span_send, span_recv, span_own, enc_send, enc_recv, enc_own = scratch[3 * chunks :]
     me_enc, me_span = lax.axis_index("enc"), lax.axis_index("span")
 
     def span_copy(c, d):
         peer = lax.rem(me_span + d, shard_count)
         return pltpu.make_async_remote_copy(
-            src_ref=in_ref.at[c, pl.ds(peer * capacity, capacity)],
+            src_ref=outgoing[c].at[pl.ds(peer * capacity, capacity)],
             dst_ref=received[c].at[pl.ds(me_span * capacity, capacity)],
             send_sem=span_send.at[c, d],
             recv_sem=span_recv.at[c, d],
@@ -95,7 +78,7 @@
 
     def span_local(c):
         here = pl.ds(me_span * capacity, capacity)
-        return pltpu.make_async_copy(in_ref.at[c, here], received[c].at[here], span_own.at[c])
+        return pltpu.make_async_copy(outgoing[c].at[here], received[c].at[here], span_own.at[c])
 
     def enc_copy(c, d):
         peer = lax.rem(me_enc + d, enc_count)
@@ -111,19 +94,37 @@
     def enc_local(c):
         return pltpu.make_async_copy(mine[c], out_ref.at[c, me_enc], enc_own.at[c])
 
-    greet(me_enc, me_span, enc_count, shard_count)
-    for c in range(chunks):
+    def pack(c):
+        def encode(p, carry):
+            b = served_ref[p]
+            wide = store_ref[b, c * rows : (c + 1) * rows].astype(jnp.float32)
+            outgoing[c][p] = (wide * scale_ref[b]).astype(jnp.bfloat16)
+            return carry
+
+        lax.fori_loop(0, slots, encode, 0, unroll=4)
+
+    def send(c):
         each(shard_count, lambda d: span_copy(c, d).start())
         span_local(c).start()
+
+    pack(0)
+    greet(me_enc, me_span, enc_count, shard_count)
+    send(0)
+    for c in range(1, chunks):
+        pack(c)
+        if c < WINDOW:
+            send(c)
     for c in range(chunks):
         each(shard_count, lambda d: span_copy(c, d).wait_recv())
         span_local(c).wait()
+        if c + WINDOW < chunks:
+            send(c + WINDOW)
 
         def pick(i, carry):
             mine[c][i] = received[c][order_ref[i]]
             return carry
 
-        lax.fori_loop(0, used, pick, 0)
+        lax.fori_loop(0, used, pick, 0, unroll=4)
         each(enc_count, lambda d: enc_copy(c, d).start())
         enc_local(c).start()
     for c in range(chunks):
@@ -187,13 +188,13 @@
             merged[c][i] = total.astype(jnp.bfloat16)
             return carry
 
-        lax.fori_loop(0, used, add, 0)
+        lax.fori_loop(0, used, add, 0, unroll=4)
 
         def put(p, carry):
             by_slot[c][p] = merged[c][place_ref[p]]
             return carry
 
-        lax.fori_loop(0, slots, put, 0)
+        lax.fori_loop(0, slots, put, 0, unroll=4)
         each(shard_count, lambda d: span_copy(c, d).start())
         span_local(c).start()
     for c in range(chunks):
@@ -214,6 +215,8 @@
     wv_ref,
     att_ref,
     part_ref,
+    key_t,
+    value_t,
     grad_k,
     grad_v,
 ):
@@ -226,49 +229,67 @@
     dims_t = (((0,), (0,)), ((), ()))
     dims_nt = (((1,), (1,)), ((), ()))
     f32 = jnp.float32
+    bf16 = jnp.bfloat16
+    lives, masks, xs = [], [], []
     for j in range(SPANS_PER_STEP):
         span = step * SPANS_PER_STEP + j
         second = valid_ref[span].astype(f32)
-        live = span < live_ref[0]
-        mask = jnp.where(cols < NT, 1.0, second)
-        halves = [
-            jnp.concatenate([x_ref[c, e, NBR * j + k] for e, c in pieces], axis=0)
-            for k in range(NBR)
+        lives.append(span < live_ref[0])
+        masks.append(jnp.where(cols < NT, 1.0, second))
+        for k in range(NBR):
+            xs.append(jnp.concatenate([x_ref[c, e, NBR * j + k] for e, c in pieces], axis=0))
+    x = jnp.concatenate(xs, axis=1)
+    key_t[...] = jnp.dot(wkt_ref[...], x, preferred_element_type=f32).astype(bf16)
+    value_t[...] = jnp.dot(wvt_ref[...], x, preferred_element_type=f32).astype(bf16)
+
+    for j0 in range(0, SPANS_PER_STEP, SPANS_TOGETHER):
+        items = []
+        for j in range(j0, j0 + SPANS_TOGETHER):
+            for h in range(heads):
+                rows = slice(j * CL, (j + 1) * CL)
+                keys = slice(j * NBR * NT, (j + 1) * NBR * NT)
+                items.append((j, rows, slice(h * HD, (h + 1) * HD), keys))
+        scores = [
+            jnp.dot(q_ref[rows, head], key_t[head, keys], preferred_element_type=f32)
+            for j, rows, head, keys in items
         ]
-        x = jnp.concatenate(halves, axis=1)
-        key_t = jnp.dot(wkt_ref[...], x, preferred_element_type=f32).astype(jnp.bfloat16)
-        value_t = jnp.dot(wvt_ref[...], x, preferred_element_type=f32).astype(jnp.bfloat16)
-        rows = slice(j * CL, (j + 1) * CL)
-        for h in range(heads):
-            head = slice(h * HD, (h + 1) * HD)
-            q = q_ref[rows, head]
-            go = c_ref[rows, head]
-            go = jnp.where(live, go, jnp.zeros_like(go))
-            k_t = key_t[head, :]
-            v_t = value_t[head, :]
-            scores = jnp.dot(q, k_t, preferred_element_type=f32) * scale_factor
-            weights = jnp.exp(scores) * mask
-            probs = weights / jnp.sum(weights, axis=1, keepdims=True)
-            low = probs.astype(jnp.bfloat16)
-            mixture = lax.dot_general(low, v_t, dims_nt, preferred_element_type=f32)
-            att_ref[rows, head] = jnp.where(live, mixture, 0.0).astype(jnp.bfloat16)
-            grad_v[j, head, :] = lax.dot_general(
-                go, low, dims_t, preferred_element_type=f32
-            ).astype(jnp.bfloat16)
-            grad_p = jnp.dot(go, v_t, preferred_element_type=f32)
-            inner = jnp.sum(probs * grad_p, axis=1, keepdims=True)
-            grad_s = (probs * (grad_p - inner) * scale_factor).astype(jnp.bfloat16)
-            grad_k[j, head, :] = lax.dot_general(
-                q, grad_s, dims_t, preferred_element_type=f32
-            ).astype(jnp.bfloat16)
-        part = jnp.dot(wk_ref[...], grad_k[j], preferred_element_type=f32)
-        part = part + jnp.dot(wv_ref[...], grad_v[j], preferred_element_type=f32)
-        part = part.astype(jnp.bfloat16)
-        for k in range(NBR):
-            for n, (e, c) in enumerate(pieces):
-                part_ref[c, e, NBR * j + k] = part[
-                    n * rows_c : (n + 1) * rows_c, k * NT : (k + 1) * NT
-                ]
+        grad_out = [
+            jnp.where(lives[j], c_ref[rows, head], jnp.zeros((CL, HD), bf16))
+            for j, rows, head, keys in items
+        ]
+        grad_p = [
+            jnp.dot(go, value_t[head, keys], preferred_element_type=f32)
+            for go, (j, rows, head, keys) in zip(grad_out, items)
+        ]
+        probs = []
+        for raw, (j, rows, head, keys) in zip(scores, items):
+            weights = jnp.exp(raw * scale_factor) * masks[j]
+            probs.append(weights / jnp.sum(weights, axis=1, keepdims=True))
+        low = [p.astype(bf16) for p in probs]
+        grad_s = []
+        for p, gp in zip(probs, grad_p):
+            inner = jnp.sum(p * gp, axis=1, keepdims=True)
+            grad_s.append((p * (gp - inner) * scale_factor).astype(bf16))
+        for pl_low, (j, rows, head, keys) in zip(low, items):
+            mixture = lax.dot_general(
+                pl_low, value_t[head, keys], dims_nt, preferred_element_type=f32
+            )
+            att_ref[rows, head] = jnp.where(lives[j], mixture, 0.0).astype(bf16)
+        for go, pl_low, (j, rows, head, keys) in zip(grad_out, low, items):
+            grad_v[head, keys] = lax.dot_general(
+                go, pl_low, dims_t, preferred_element_type=f32
+            ).astype(bf16)
+        for gs, (j, rows, head, keys) in zip(grad_s, items):
+            grad_k[head, keys] = lax.dot_general(
+                q_ref[rows, head], gs, dims_t, preferred_element_type=f32
+            ).astype(bf16)
+
+    part = jnp.dot(wk_ref[...], grad_k[...], preferred_element_type=f32)
+    part = part + jnp.dot(wv_ref[...], grad_v[...], preferred_element_type=f32)
+    part = part.astype(bf16)
+    for b in range(SPANS_PER_STEP * NBR):
+        for n, (e, c) in enumerate(pieces):
+            part_ref[c, e, b] = part[n * rows_c : (n + 1) * rows_c, b * NT : (b + 1) * NT]
 
 
 def gather_kernel(served_ref, in_ref, scale_ref, out_ref, total):
@@ -285,8 +306,7 @@
     lax.fori_loop(0, slots, add, 0)
 
     def write(b, carry):
-        scaled = total[b] * scale_ref[pl.ds(b, 1), :]
-        out_ref[b] = scaled.T
+        out_ref[b] = total[b] * scale_ref[b]
         return carry
 
     lax.fori_loop(0, out_ref.shape[0], write, 0)
@@ -313,7 +333,8 @@
     used_count = slot_order.shape[0]
     spans = used_count // NBR
     served = fetch_index[0].reshape(slot_total)
-    scale_wide = block_scale.astype(jnp.float32)
+    scale_wide = block_scale.astype(jnp.float32)[:, None, :]
+    store_rows = neighbour_store.transpose(0, 2, 1)
     bf16 = jnp.bfloat16
     rows = features // CHUNKS
     used_index = jnp.arange(used_count, dtype=jnp.int32)
@@ -321,14 +342,6 @@
     named = slot_order[None, :] == slot_index[:, None]
     place = jnp.min(jnp.where(named, used_index[None, :], used_count), axis=1)
 
-    outgoing = pl.pallas_call(
-        pack_kernel,
-        out_shape=jax.ShapeDtypeStruct((CHUNKS, slot_total, rows, NT), bf16),
-        in_specs=[SMEM, VMEM, VMEM],
-        out_specs=VMEM,
-        scratch_shapes=[pltpu.VMEM((blocks_here, features, NT), bf16)],
-        compiler_params=params(),
-    )(served, neighbour_store, scale_wide)
     dma = pltpu.SemaphoreType.DMA
     semaphores = [
         dma((CHUNKS, shard_count)),
@@ -341,13 +354,13 @@
     whole = pl.pallas_call(
         functools.partial(fetch_kernel, enc_count, shard_count),
         out_shape=jax.ShapeDtypeStruct((CHUNKS, enc_count, used_count, rows, NT), bf16),
-        in_specs=[SMEM, VMEM],
+        in_specs=[SMEM, SMEM, VMEM, VMEM],
         out_specs=ANY,
-        scratch_shapes=[pltpu.VMEM((slot_total, rows, NT), bf16)] * CHUNKS
+        scratch_shapes=[pltpu.VMEM((slot_total, rows, NT), bf16)] * (2 * CHUNKS)
         + [pltpu.VMEM((used_count, rows, NT), bf16)] * CHUNKS
         + semaphores,
         compiler_params=params(collective_id=0, has_side_effects=True),
-    )(slot_order, outgoing)
+    )(slot_order, served, store_rows, scale_wide)
 
     step_blocks = SPANS_PER_STEP * NBR
     step_rows = SPANS_PER_STEP * CL
@@ -376,9 +389,9 @@
             ],
             out_specs=[by_rows, by_blocks],
             scratch_shapes=[
-                pltpu.VMEM((SPANS_PER_STEP, head_width, NBR * NT), bf16),
-                pltpu.VMEM((SPANS_PER_STEP, head_width, NBR * NT), bf16),
-            ],
+                pltpu.VMEM((head_width, step_blocks * NT), bf16),
+            ]
+            * 4,
         ),
         compiler_params=params(dimension_semantics=("arbitrary",)),
     )(
@@ -406,13 +419,13 @@
     )(place, partial)
     grad_store = pl.pallas_call(
         gather_kernel,
-        out_shape=jax.ShapeDtypeStruct(neighbour_store.shape, jnp.float32),
+        out_shape=jax.ShapeDtypeStruct(store_rows.shape, jnp.float32),
         in_specs=[SMEM, VMEM, VMEM],
         out_specs=VMEM,
         scratch_shapes=[pltpu.VMEM((blocks_here, features, NT), jnp.float32)],
         compiler_params=params(),
     )(served, arrived, scale_wide)
-    return (attended, grad_store)
+    return (attended, grad_store.transpose(0, 2, 1))
 
 
 def solution(mesh):

time: 310 us -> 259 us (0.84)
  Pallas kernels: 291 us -> 249 us
  local copies, waits for them, and re-layouts: 13.9 us -> 4.49 us
    pallas_call x1, Pallas kernels: 59.8 us -> 39.5 us  [per_device(): pl.pallas_call(attend_kernel, out_shape=(jax.ShapeDtypeStruct(queries.sha...]
    pallas_call x1, Pallas kernels: 117 us -> 106 us  [per_device(): pl.pallas_call(functools.partial(fetch_kernel, enc_count, shard_count), o...]
    pallas_call x2 -> x1, Pallas kernels: 15.7 us -> 5.44 us  [per_device(): pl.pallas_call(gather_kernel, out_shape=jax.ShapeDtypeStruct(store_rows.s...]
    unnamed x10 -> x8, local copies, waits for them, and re-layouts: 12.6 us -> 3.16 us
where the time goes in v3:
time: 259 us; the launch traced here: 256 us
  Pallas kernels  249 us (96%)
  local copies, waits for them, and re-layouts  4.49 us (2%)
    pallas_call x1, Pallas kernels, per_device(): pl.pallas_call(functools.partial(fetch_kernel, enc_count, shard_count), o...  106 us
    pallas_call x1, Pallas kernels, per_device(): pl.pallas_call(functools.partial(return_kernel, enc_count, shard_count),...  97.8 us
    pallas_call x1, Pallas kernels, per_device(): pl.pallas_call(attend_kernel, out_shape=(jax.ShapeDtypeStruct(queries.sha...  39.5 us
    pallas_call x1, Pallas kernels, per_device(): pl.pallas_call(gather_kernel, out_shape=jax.ShapeDtypeStruct(store_rows.s...  5.44 us

profile of v3, /device:TPU:0, one launch (start us, length us, event | category | flops | bytes accessed | tf_op | source)
XLA Modules:
  0.0 256.4 jit_solution(8984357153446805652)
XLA Ops:
  0.6 1.3 broadcast_in_dim.23
  1.9 1.3 reshape_squeeze.3.served_ref
  3.3 0.0 copy-start
  3.3 105.9 %shard_map.113.x_ref = bf16[7,4,32,32,128]{4,3,2,1,0:T(8,128)(2,1)} custom-call(s32[32]{0:T(128)} %bitcast.14, s32[64]{0:T(128)} %reshape_squeeze.3.served_ref, bf16[32,224,128]{2,1,0:T(8,128)(2,1)} %bitcast.10, f32[32,1,128]{2,1,0:T(1,128)} %bitcast.11), custom_call_target="tpu_custom_call" | custom-call | tf_op jit(solution)/shard_map/pallas_call | solution.py:354
  109.2 0.0 copy-done
  109.2 0.0 copy-start.1
  109.2 1.6 copy.14
  110.8 0.0 copy-done.1
  110.8 1.6 copy.15
  113.0 0.0 copy-start.2
  113.0 39.5 %shard_map.114 = (bf16[1024,768]{1,0:T(8,128)(2,1)}, bf16[7,4,32,32,128]{4,3,2,1,0:T(8,128)(2,1)}) custom-call(s32[16]{0:T(128)} %bitcast.13, s32[1]{0:T(128)S(6)} %copy.16.live_ref, bf16[7,4,32,32,128]{4,3,2,1,0:T(8,128)(2,1)} %shard_map.113.x_ref, bf16[1024,768]{1,0:T(8,128)(2,1)} %q_ref.1, bf16[1024,768]{1,0:T(8,128)(2,1)} %c_ref.1, ...), custom_call_target="tpu_custom_call" | custom-call | tf_op jit(solution)/shard_map/pallas_call | solution.py:372
  152.5 0.0 copy-done.2
  152.5 0.6 select_reduce_fusion.place_ref
  153.1 97.8 %shard_map.115.in_ref = bf16[7,64,32,128]{3,2,1,0:T(8,128)(2,1)} custom-call(s32[64]{0:T(128)} %select_reduce_fusion.place_ref, bf16[7,4,32,32,128]{4,3,2,1,0:T(8,128)(2,1)} %get-tuple-element.5.in_ref), custom_call_target="tpu_custom_call" | custom-call | tf_op jit(solution)/shard_map/pallas_call | solution.py:409
  251.0 5.4 %shard_map.116 = f32[32,224,128]{2,1,0:T(8,128)} custom-call(s32[64]{0:T(128)} %reshape_squeeze.3.served_ref, bf16[7,64,32,128]{3,2,1,0:T(8,128)(2,1)} %shard_map.115.in_ref, f32[32,1,128]{2,1,0:T(1,128)} %bitcast.12), custom_call_target="tpu_custom_call" | custom-call | tf_op jit(solution)/shard_map/pallas_call | solution.py:420
Async XLA Ops:
  3.3 106.0 %copy-start = (bf16[896,768]{1,0:T(8,128)(2,1)S(1)}, bf16[896,768]{1,0:T(8,128)(2,1)}, u32[]{:S(2)}) copy-start(bf16[896,768]{1,0:T(8,128)(2,1)} %wk_ref.1) | copy-start | bytes 4128772
  109.2 1.6 copy-start.1
  113.0 39.5 %copy-start.2 = (s32[1,32]{1,0:T(1,128)S(1)}, s32[1,32]{1,0:T(1,128)}, u32[]{:S(2)}) copy-start(s32[1,32]{1,0:T(1,128)} %param.17) | copy-start | bytes 388

commit v4 on v3

--- a/solution.py
+++ b/solution.py
@@ -13,9 +13,10 @@
 NT = 128
 NBR = 2
 SPANS_PER_STEP = 2
-SPANS_TOGETHER = 1
-CHUNKS = 7
-WINDOW = 1
+SPANS_TOGETHER = 2
+CHUNKS = 14
+WINDOW = 2
+ENC_WINDOW = 2
 MESH = pl.DeviceIdType.MESH
 VMEM_BYTES = 56 * 1024 * 1024
 
@@ -173,12 +174,18 @@
         return pltpu.make_async_copy(by_slot[c].at[here], out_ref.at[c, here], span_own.at[c])
 
     greet(me_enc, me_span, enc_count, shard_count)
-    for c in range(chunks):
+
+    def send(c):
         each(enc_count, lambda d: enc_copy(c, d).start())
         enc_local(c).start()
+
+    for c in range(min(ENC_WINDOW, chunks)):
+        send(c)
     for c in range(chunks):
         each(enc_count, lambda d: enc_copy(c, d).wait_recv())
         enc_local(c).wait()
+        if c + ENC_WINDOW < chunks:
+            send(c + ENC_WINDOW)
         merged[c][used] = jnp.zeros(merged[c].shape[1:], jnp.bfloat16)
 
         def add(i, carry):
@@ -209,8 +216,6 @@
     x_ref,
     q_ref,
     c_ref,
-    wkt_ref,
-    wvt_ref,
     wk_ref,
     wv_ref,
     att_ref,
@@ -219,6 +224,8 @@
     value_t,
     grad_k,
     grad_v,
+    wkt_ref,
+    wvt_ref,
 ):
     step = pl.program_id(0)
     heads = q_ref.shape[1] // HD
@@ -230,6 +237,12 @@
     dims_nt = (((1,), (1,)), ((), ()))
     f32 = jnp.float32
     bf16 = jnp.bfloat16
+
+    @pl.when(step == 0)
+    def _():
+        wkt_ref[...] = wk_ref[...].T
+        wvt_ref[...] = wv_ref[...].T
+
     lives, masks, xs = [], [], []
     for j in range(SPANS_PER_STEP):
         span = step * SPANS_PER_STEP + j
@@ -382,8 +395,6 @@
                 by_blocks,
                 by_rows,
                 by_rows,
-                pl.BlockSpec((head_width, enc_features), resident),
-                pl.BlockSpec((head_width, enc_features), resident),
                 pl.BlockSpec((enc_features, head_width), resident),
                 pl.BlockSpec((enc_features, head_width), resident),
             ],
@@ -391,7 +402,8 @@
             scratch_shapes=[
                 pltpu.VMEM((head_width, step_blocks * NT), bf16),
             ]
-            * 4,
+            * 4
+            + [pltpu.VMEM((head_width, enc_features), bf16)] * 2,
         ),
         compiler_params=params(dimension_semantics=("arbitrary",)),
     )(
@@ -400,8 +412,6 @@
         whole,
         queries,
         cotangent,
-        key_weight.T,
-        value_weight.T,
         key_weight,
         value_weight,
     )

time: 259 us -> 248 us (0.958)
  Pallas kernels: 249 us -> 243 us
  local copies, waits for them, and re-layouts: 4.49 us -> 1.37 us
    pallas_call x1, Pallas kernels: 106 us -> 101 us  [per_device(): pl.pallas_call(functools.partial(fetch_kernel, enc_count, shard_count), o...]
    unnamed x8 -> x2, local copies, waits for them, and re-layouts: 3.16 us -> 0.01 us
where the time goes in v4:
time: 248 us
  Pallas kernels  243 us (98%)
    pallas_call x1, Pallas kernels, per_device(): pl.pallas_call(functools.partial(fetch_kernel, enc_count, shard_count), o...  101 us
    pallas_call x1, Pallas kernels, per_device(): pl.pallas_call(functools.partial(return_kernel, enc_count, shard_count),...  98.2 us
    pallas_call x1, Pallas kernels, per_device(): pl.pallas_call(attend_kernel, out_shape=(jax.ShapeDtypeStruct(queries.sha...  38.7 us
    pallas_call x1, Pallas kernels, per_device(): pl.pallas_call(gather_kernel, out_shape=jax.ShapeDtypeStruct(store_rows.s...  5.5 us

profile of v4, /device:TPU:0, one launch (start us, length us, event | category | flops | bytes accessed | tf_op | source)
XLA Modules:
  0.0 247.6 jit_solution(8366481123756250690)
XLA Ops:
  0.6 1.3 broadcast_in_dim.23
  1.9 1.4 reshape_squeeze.3.served_ref
  3.3 100.8 %shard_map.113.x_ref = bf16[14,4,32,16,128]{4,3,2,1,0:T(8,128)(2,1)} custom-call(s32[32]{0:T(128)} %bitcast.9, s32[64]{0:T(128)} %reshape_squeeze.3.served_ref, bf16[32,224,128]{2,1,0:T(8,128)(2,1)} %bitcast.6, f32[32,1,128]{2,1,0:T(1,128)} %bitcast.7), custom_call_target="tpu_custom_call" | custom-call | tf_op jit(solution)/shard_map/pallas_call | solution.py:367
  104.7 0.0 copy-start
  104.7 38.7 %shard_map.114 = (bf16[1024,768]{1,0:T(8,128)(2,1)}, bf16[14,4,32,16,128]{4,3,2,1,0:T(8,128)(2,1)}) custom-call(s32[16]{0:T(128)} %bitcast.11, s32[1]{0:T(128)S(6)} %copy.12.live_ref, bf16[14,4,32,16,128]{4,3,2,1,0:T(8,128)(2,1)} %shard_map.113.x_ref, bf16[1024,768]{1,0:T(8,128)(2,1)} %q_ref.1, bf16[1024,768]{1,0:T(8,128)(2,1)} %c_ref.1, ...), custom_call_target="tpu_custom_call" | custom-call | tf_op jit(solution)/shard_map/pallas_call | solution.py:385
  143.4 0.0 copy-done
  143.4 0.6 select_reduce_fusion.place_ref
  144.0 98.2 %shard_map.115.in_ref = bf16[14,64,16,128]{3,2,1,0:T(8,128)(2,1)} custom-call(s32[64]{0:T(128)} %select_reduce_fusion.place_ref, bf16[14,4,32,16,128]{4,3,2,1,0:T(8,128)(2,1)} %get-tuple-element.5.in_ref), custom_call_target="tpu_custom_call" | custom-call | tf_op jit(solution)/shard_map/pallas_call | solution.py:419
  242.1 5.5 %shard_map.116 = f32[32,224,128]{2,1,0:T(8,128)} custom-call(s32[64]{0:T(128)} %reshape_squeeze.3.served_ref, bf16[14,64,16,128]{3,2,1,0:T(8,128)(2,1)} %shard_map.115.in_ref, f32[32,1,128]{2,1,0:T(1,128)} %bitcast.8), custom_call_target="tpu_custom_call" | custom-call | tf_op jit(solution)/shard_map/pallas_call | solution.py:430
Async XLA Ops:
  104.7 38.7 %copy-start = (s32[1,32]{1,0:T(1,128)S(1)}, s32[1,32]{1,0:T(1,128)}, u32[]{:S(2)}) copy-start(s32[1,32]{1,0:T(1,128)} %param.17) | copy-start | bytes 388
